TPU v7x, 256 devices: a whole 4x4x8 slice. The times are simulated.
256 devices in a mesh: replica: 4 (over y_lo, core), fsdp: 64 (over z, x, y_hi).
Axes of the slice: x: 4, y: 4 (y_hi: 2, y_lo: 2; y = y_hi * 2 + y_lo), z: 8, core: 2. Of those that a mesh axis runs over, the one named last changes fastest.
Arguments:
- features: bfloat16 [4, 2, 16384, 2304], P('replica', None, 'fsdp'), may hold values from -6 to 6
- queries: bfloat16 [4, 2, 16384, 2048], P('replica', None, 'fsdp'), may hold values from -6 to 6
- values: bfloat16 [4, 2, 16384, 1024], P('replica', None, 'fsdp'), may hold values from -6 to 6
- out_grad: bfloat16 [4, 2, 16384, 2048], P('replica', None, 'fsdp'), may hold values from -6 to 6
- doc_ids: int32 [4, 2, 16384], P('replica', None, 'fsdp'), may hold values from 0 to 255, never falling along the last dimension, each value on 1 to 256 neighbouring positions
- fragment: int32 [1], replicated, may hold values from 0 to 16383
- local_weight: float32 [4, 2304, 1024], P('replica', 'fsdp'), may hold values from -6 to 6
- first_moment: float32 [4, 2304, 1024], P('replica', 'fsdp'), may hold values from -1.5 to 1.5
- second_moment: float32 [4, 2304, 1024], P('replica', 'fsdp'), may hold values from 0.01 to 1
- global_weight: float32 [2304, 1024], P('fsdp'), may hold values from -6 to 6
- outer_momentum: float32 [2304, 1024], P('fsdp'), may hold values from -4 to 4
- outer_delta: float32 [4, 2304, 1024], P('replica', 'fsdp'), may hold values from -4 to 4
Outputs:
- new_local: float32 [4, 2304, 1024], P('replica', 'fsdp')
- new_first: float32 [4, 2304, 1024], P('replica', 'fsdp')
- new_second: float32 [4, 2304, 1024], P('replica', 'fsdp')
- new_global: float32 [2304, 1024], P('fsdp')
- new_momentum: float32 [2304, 1024], P('fsdp')
Inputs may be any that keep to these rules, and one draw needn't show every extreme that they name: `doc_ids`: document numbers never fall along the tokens of a replica and step; a document holds 1 to 256 tokens.
All inputs are finite; a program needn't handle non-finite values.
Results may differ from a plain program's by a relative error of at most 0.008.
Values may be sent and summed in bfloat16 or wider, within the bound.
No kernel may reach another device: no remote copies, remote signals or barrier semaphores. Data moves between devices by JAX's collectives and lax.ppermute only.
A program may use at most 128 MiB of HBM per device.

v0:
```python
import jax
import jax.numpy as jnp
from jax import lax
from jax.sharding import PartitionSpec as P

HEAD = 128
STEPS = 2
FRAGS = 4


LEARN_RATE = 0.1
DECAY_RATE = 0.1
BETA_ONE = 0.9
BETA_TWO = 0.999
EPSILON = 1e-08
OUTER_MU = 0.9
OUTER_RATE = 0.7
MERGE_RATE = 0.5
SOFT_CAP = 50.0
QUERY_SCALE = 1.0 / 12.0


def key_cotangent(queries, keys, values, out_grad, docs):
    length = queries.shape[0]
    kv_heads = keys.shape[1] // HEAD
    group = queries.shape[1] // keys.shape[1]
    query_heads = queries.reshape(length, kv_heads, group, HEAD)
    key_heads = keys.reshape(length, kv_heads, HEAD)
    value_heads = values.reshape(length, kv_heads, HEAD)
    grad_heads = out_grad.reshape(length, kv_heads, group, HEAD)
    raw = (
        jnp.einsum("ikgd,jkd->kgij", query_heads, key_heads, preferred_element_type=jnp.float32)
        * QUERY_SCALE
    )
    capped = jnp.tanh(raw / SOFT_CAP)
    places = jnp.arange(length)
    allowed = (places[None, :] <= places[:, None]) & (docs[:, None] == docs[None, :])
    expo = jnp.where(allowed, jnp.exp(SOFT_CAP * capped), jnp.float32(0.0))
    probs = expo / jnp.sum(expo, axis=-1, keepdims=True)
    dprob = jnp.einsum(
        "ikgd,jkd->kgij", grad_heads, value_heads, preferred_element_type=jnp.float32
    )
    inner = jnp.sum(probs * dprob, axis=-1, keepdims=True)
    dscore = (probs * (dprob - inner) * (1.0 - capped * capped)).astype(jnp.bfloat16)
    dkeys = (
        jnp.einsum("kgij,ikgd->jkd", dscore, query_heads, preferred_element_type=jnp.float32)
        * QUERY_SCALE
    )
    return dkeys.reshape(length, kv_heads * HEAD).astype(jnp.bfloat16)


def outer_merge(fragment, global_weight, outer_momentum, outer_delta):
    frag_cols = global_weight.shape[1] // FRAGS
    start = fragment[0] % FRAGS * frag_cols
    piece = lax.dynamic_slice_in_dim(outer_delta[0], start, frag_cols, 1)
    old_global = lax.dynamic_slice_in_dim(global_weight, start, frag_cols, 1)
    old_moment = lax.dynamic_slice_in_dim(outer_momentum, start, frag_cols, 1)
    mean = lax.psum(piece, "replica") / lax.axis_size("replica")
    fresh_moment = OUTER_MU * old_moment + mean
    fresh_global = old_global - OUTER_RATE * (mean + OUTER_MU * fresh_moment)
    new_global = lax.dynamic_update_slice_in_dim(global_weight, fresh_global, start, 1)
    new_momentum = lax.dynamic_update_slice_in_dim(outer_momentum, fresh_moment, start, 1)
    return (start, fresh_global, new_global, new_momentum)


def weight_term(inputs, dkeys, factor):
    product = lax.dot_general(
        inputs, dkeys, (((0,), (0,)), ((), ())), preferred_element_type=jnp.float32
    )
    return product * factor


def on_device(
    features,
    queries,
    values,
    out_grad,
    doc_ids,
    fragment,
    local_weight,
    first_moment,
    second_moment,
    global_weight,
    outer_momentum,
    outer_delta,
):
    factor = features.shape[-1] ** (-0.5)
    weight = local_weight[0]
    moment = first_moment[0]
    second = second_moment[0]
    groups = lax.axis_size("fsdp")
    for step in range(STEPS):
        inputs = features[0, step]
        shard = weight.astype(jnp.bfloat16)
        owned = shard.shape[0]
        summed_keys = jnp.dot(
            inputs,
            lax.all_gather(shard, "fsdp", axis=0, tiled=True),
            preferred_element_type=jnp.float32,
        )
        keys = (summed_keys * factor).astype(jnp.bfloat16)
        dkeys = key_cotangent(
            queries[0, step], keys, values[0, step], out_grad[0, step], doc_ids[0, step]
        )
        whole_term = weight_term(inputs, dkeys, factor)
        arrived = lax.all_to_all(whole_term, "fsdp", split_axis=0, concat_axis=0, tiled=True)
        grad = jnp.sum(arrived.reshape(groups, owned, whole_term.shape[1]), axis=0)
        moment = BETA_ONE * moment + (1.0 - BETA_ONE) * grad
        second = BETA_TWO * second + (1.0 - BETA_TWO) * grad * grad
        weight = weight - LEARN_RATE * (moment / (jnp.sqrt(second) + EPSILON) + DECAY_RATE * weight)
    outcome = outer_merge(fragment, global_weight, outer_momentum, outer_delta)
    start, fresh_global, new_global, new_momentum = outcome
    frag_cols = fresh_global.shape[1]
    local_frag = lax.dynamic_slice_in_dim(weight, start, frag_cols, 1)
    merged = MERGE_RATE * local_frag + (1.0 - MERGE_RATE) * fresh_global
    weight = lax.dynamic_update_slice_in_dim(weight, merged, start, 1)
    return (weight[None], moment[None], second[None], new_global, new_momentum)


def solution(mesh):
    placed = (
        P("replica", None, "fsdp", None),
        P("replica", None, "fsdp", None),
        P("replica", None, "fsdp", None),
        P("replica", None, "fsdp", None),
        P("replica", None, "fsdp"),
        P(),
        P("replica", "fsdp", None),
        P("replica", "fsdp", None),
        P("replica", "fsdp", None),
        P("fsdp", None),
        P("fsdp", None),
        P("replica", "fsdp", None),
    )
    return jax.shard_map(
        on_device,
        mesh=mesh,
        in_specs=placed,
        out_specs=(
            P("replica", "fsdp", None),
            P("replica", "fsdp", None),
            P("replica", "fsdp", None),
            P("fsdp", None),
            P("fsdp", None),
        ),
        check_vma=False,
    )
```

profile of v0, /device:TPU:26, one launch (start us, length us, event | category | flops | bytes accessed | tf_op | source)
XLA Modules:
  0.0 877.8 jit_solution(15675265381062298130)
XLA Ops:
  7.2 0.0 copy-start
  7.2 0.0 all-gather.5.cloned.1.call-start
  7.2 1.6 copy.160
  8.9 1.6 copy.161
  10.4 1.6 copy.152
  12.0 0.0 all-gather.5.cloned.1.call-update
  12.0 0.0 all-gather.7.cloned.1.call-start
  12.1 1.7 fusion.81
  13.8 0.5 copy.102
  14.3 0.0 copy-start.12
  14.3 2.7 fusion.80
  17.1 2.3 copy.104
  19.3 2.3 fusion.82
  21.6 2.1 copy.103
  23.7 0.1 fusion.46
  23.8 4.2 fusion.84
  28.0 117.5 %all-gather.5.cloned.1.call-done = bf16[64,36,1024]{2,1,0:T(8,128)(2,1)} async-done(((bf16[1,36,1024]{2,1,0:T(8,128)(2,1)}), bf16[64,36,1024]{2,1,0:T(8,128)(2,1)}) %all-gather.5.cloned.1.call-update) | async-done | bytes 4718608 | tf_op jit(solution)/shard_map/all_gather | solution.py:98
  145.4 7.2 reshape.82
  152.6 4.1 fusion.32
  156.7 0.1 copy.108
  156.9 0.8 copy-done.1
  157.7 2.7 fusion.41
  160.4 4.8 fusion.8
  165.1 9.7 %fusion.29 = bf16[8,256,128]{1,2,0:T(8,128)(2,1)} fusion(bf16[256,8,2,128]{0,3,2,1:T(8,128)(2,1)S(1)} %bitcast.230, f32[8,2,256,256]{2,3,1,0:T(8,128)} %fusion.8, f32[8,256,256,2]{2,1,3,0:T(8,128)} %fusion.84, f32[8,256,256,2]{2,1,3,0:T(8,128)} %fusion.41), kind=kOutput, calls=%fused_computation.43 | convolution fusion | flops 277352704 | bytes 14155776 | tf_op jit(solution)/shard_map/kgij,ikgd->jkd/dot_general | solution.py:46
  174.8 6.4 multiply_bitcast_fusion.1
  181.3 9.6 %copy.64 = f32[2304,1024]{1,0:T(8,128)} copy(f32[2304,1024]{0,1:T(8,128)} %multiply_bitcast_fusion.1) | data formatting | bytes 18874368 | tf_op jit(solution)/shard_map/mul | solution.py:70
  190.8 9.9 %all_to_all.12 = f32[64,36,1024]{2,1,0:T(8,128)} reshape(f32[2304,1024]{1,0:T(8,128)} %copy.64) | data formatting | bytes 18874368 | tf_op jit(solution)/shard_map/all_to_all | solution.py:106
  200.7 237.5 %all_to_all.18 = f32[64,36,1024]{2,1,0:T(8,128)} all-to-all(f32[64,36,1024]{2,1,0:T(8,128)} %all_to_all.12), channel_id=1, replica_groups=mesh['replica'=4,'fsdp'=64] {'fsdp'}, dimensions={0} | all-to-all | bytes 18874368 | tf_op jit(solution)/shard_map/all_to_all | solution.py:106
  438.2 4.7 reduce_sum.60
  443.0 0.0 copy-done.4
  443.0 0.0 copy-done.6
  443.0 0.9 convert_bitcast_fusion
  443.9 0.0 all-gather.7.cloned.1.call-update
  443.9 0.5 copy.105
  444.4 0.5 copy.107
  445.0 1.2 copy.106
  446.2 0.1 fusion.45
  446.3 2.8 fusion.86
  449.2 122.2 %all-gather.7.cloned.1.call-done = bf16[64,36,1024]{2,1,0:T(8,128)(2,1)} async-done(((bf16[1,36,1024]{2,1,0:T(8,128)(2,1)}), bf16[64,36,1024]{2,1,0:T(8,128)(2,1)}) %all-gather.7.cloned.1.call-update) | async-done | bytes 4718608 | tf_op jit(solution)/shard_map/all_gather | solution.py:98
  571.3 7.2 reshape.84
  578.5 4.1 fusion.31
  582.6 2.7 fusion.85
  585.4 3.7 fusion.10
  589.1 8.9 %fusion.28 = bf16[8,256,128]{1,2,0:T(8,128)(2,1)S(1)} fusion(bf16[256,8,2,128]{0,3,2,1:T(8,128)(2,1)S(1)} %bitcast.233, f32[8,2,256,256]{2,3,1,0:T(8,128)} %fusion.10, f32[8,256,256,2]{2,1,3,0:T(8,128)} %fusion.86, f32[8,256,256,2]{2,1,3,0:T(8,128)} %fusion.85), kind=kOutput, calls=%fused_computation.42 | convolution fusion | flops 277352704 | bytes 14155776 | tf_op jit(solution)/shard_map/kgij,ikgd->jkd/dot_general | solution.py:46
  598.0 6.3 multiply_bitcast_fusion
  604.3 9.6 %copy.76 = f32[2304,1024]{1,0:T(8,128)} copy(f32[2304,1024]{0,1:T(8,128)} %multiply_bitcast_fusion) | data formatting | bytes 18874368 | tf_op jit(solution)/shard_map/mul | solution.py:70
  613.8 9.9 %all_to_all.14 = f32[64,36,1024]{2,1,0:T(8,128)} reshape(f32[2304,1024]{1,0:T(8,128)} %copy.76) | data formatting | bytes 18874368 | tf_op jit(solution)/shard_map/all_to_all | solution.py:106
  623.7 10.2 %all-to-all-start.1 = ((f32[64,36,1024]{2,1,0:T(8,128)}), f32[64,36,1024]{2,1,0:T(8,128)}, u32[]{:S(2)}, u32[]{:S(2)}) async-start(f32[64,36,1024]{2,1,0:T(8,128)} %all_to_all.14), calls=%async_computation.1 | async-start | bytes 20971520 | tf_op jit(solution)/shard_map/all_to_all | solution.py:106
  634.7 29.9 %psum.7 = f32[36,256]{1,0:T(8,128)S(1)} all-reduce(f32[36,256]{1,0:T(8,128)S(1)} %bitcast.244), channel_id=1, replica_groups=mesh['replica'=4,'fsdp'=64] {'replica'}, use_global_device_ids=true, to_apply=%region_6.7 | all-reduce | flops 9216 | bytes 73728 | tf_op jit(solution)/shard_map/psum | solution.py:58
  664.6 0.0 copy-start.3
  664.6 0.0 copy-start.5
  664.6 0.0 copy-start.7
  664.6 0.0 copy-start.8
  664.6 0.0 copy-start.10
  664.7 197.8 %all-to-all-done.1 = f32[64,36,1024]{2,1,0:T(8,128)} async-done(((f32[64,36,1024]{2,1,0:T(8,128)}), f32[64,36,1024]{2,1,0:T(8,128)}, u32[]{:S(2)}, u32[]{:S(2)}) %all-to-all-start.1) | async-done | bytes 9437216 | tf_op jit(solution)/shard_map/all_to_all | solution.py:106
  862.5 4.7 reduce_sum.64
  867.2 0.3 fusion.53
  867.5 0.1 fusion.54
  867.6 0.9 bitcast_dynamic-update-slice_fusion
  868.4 0.8 copy.77
  869.3 0.0 copy-start.9
  869.3 0.0 copy-start.11
  869.3 0.8 copy.78
  870.1 0.8 copy.79
  (18 shorter events, 0.1 us)
Async XLA Ops:
  7.2 627.4 %copy-start = (f32[1,36,1024]{2,0,1:T(1,128)S(1)}, f32[1,36,1024]{2,0,1:T(1,128)}, u32[]{:S(2)}) copy-start(f32[1,36,1024]{2,0,1:T(1,128)} %param.23) | copy-start | bytes 442372
  7.2 138.3 %all-gather.5.cloned.1.call-start = ((), (), s32[]{:S(2)}) async-start(), calls=%async_computation.2 | async-start | bytes 5324800 | tf_op jit(solution)/shard_map/all_gather | solution.py:98
  12.0 559.3 %all-gather.7.cloned.1.call-start = ((), (), s32[]{:S(2)}) async-start(), calls=%async_computation.3 | async-start | bytes 5324800 | tf_op jit(solution)/shard_map/all_gather | solution.py:98
  14.3 9.3 %copy-start.12 = (s32[1,2,256]{2,1,0:T(2,128)S(1)}, s32[1,2,256]{2,1,0:T(2,128)}, u32[]{:S(2)}) copy-start(s32[1,2,256]{2,1,0:T(2,128)} %param.16) | copy-start | bytes 6148
  156.8 0.8 copy-start.1
  438.2 4.8 copy-start.2
  438.2 4.8 copy-start.4
  438.2 4.8 copy-start.6
  623.7 238.8 %all-to-all-start.1 = ((f32[64,36,1024]{2,1,0:T(8,128)}), f32[64,36,1024]{2,1,0:T(8,128)}, u32[]{:S(2)}, u32[]{:S(2)}) async-start(f32[64,36,1024]{2,1,0:T(8,128)} %all_to_all.14), calls=%async_computation.1 | async-start | bytes 20971520 | tf_op jit(solution)/shard_map/all_to_all | solution.py:106
  664.6 202.6 %copy-start.3 = (f32[1,36,1024]{2,0,1:T(1,128)S(1)}, f32[1,36,1024]{2,0,1:T(1,128)}, u32[]{:S(2)}) copy-start(f32[1,36,1024]{2,0,1:T(1,128)} %param.20) | copy-start | bytes 442372
  664.6 202.6 %copy-start.5 = (f32[1,36,1024]{2,0,1:T(1,128)S(1)}, f32[1,36,1024]{2,0,1:T(1,128)}, u32[]{:S(2)}) copy-start(f32[1,36,1024]{2,0,1:T(1,128)} %param.18) | copy-start | bytes 442372
  664.6 202.6 %copy-start.7 = (f32[1,36,1024]{2,0,1:T(1,128)S(1)}, f32[1,36,1024]{2,0,1:T(1,128)}, u32[]{:S(2)}) copy-start(f32[1,36,1024]{2,0,1:T(1,128)} %param.19) | copy-start | bytes 442372
  664.6 202.9 %copy-start.8 = (f32[36,1024]{1,0:T(8,128)S(1)}, f32[36,1024]{1,0:T(8,128)}, u32[]{:S(2)}) copy-start(f32[36,1024]{1,0:T(8,128)} %copy.160) | copy-start | bytes 442372
  664.6 202.9 %copy-start.10 = (f32[36,1024]{1,0:T(8,128)S(1)}, f32[36,1024]{1,0:T(8,128)}, u32[]{:S(2)}) copy-start(f32[36,1024]{1,0:T(8,128)} %copy.161) | copy-start | bytes 442372
  869.3 1.7 copy-start.9
  869.3 1.6 copy-start.11
Sparse Core Ops, SparseCore 0:
  12.2 133.2 all-gather.4
  444.0 127.2 all-gather.6
where the time goes:
time: 879 us; the launch traced here: 878 us
  waiting for transfers between devices  438 us (50%)
  blocking collectives  267 us (30%)
  local copies, waits for them, and re-layouts  75.3 us (9%)
  matrix products  60.5 us (7%)
  between operations  15 us (2%)
  other arithmetic  11.7 us (1%)
  starting transfers between devices  10.3 us (1%)
    all_gather x2, waiting for transfers between devices, on_device(): lax.all_gather(shard, 'fsdp', axis=0, tiled=True)  240 us
    all_to_all x1, blocking collectives, on_device(): lax.all_to_all(whole_term, 'fsdp', split_axis=0, concat_axis=0, tiled=True)  238 us
    all_to_all x1, waiting for transfers between devices, on_device(): lax.all_to_all(whole_term, 'fsdp', split_axis=0, concat_axis=0, tiled=True)  198 us
    psum x1, blocking collectives, outer_merge(): mean = lax.psum(piece, 'replica') / lax.axis_size('replica')  29.9 us
    unnamed x42, local copies, waits for them, and re-layouts  29.7 us
    all_to_all x2, local copies, waits for them, and re-layouts, on_device(): lax.all_to_all(whole_term, 'fsdp', split_axis=0, concat_axis=0, tiled=True)  19.8 us
    mul x2, local copies, waits for them, and re-layouts, weight_term(): return product * factor  19.1 us
    dot_general x2, matrix products, key_cotangent(): jnp.einsum('kgij,ikgd->jkd', dscore, query_heads, preferred_element_type=...  18.6 us
  transfers between devices with their start and end apart: 3, of which 3 were waited for; matrix products, arithmetic and copies ran while one was open for 2% of the time, Pallas kernels for 0%

commit v1 on v0

v1 whole, which is shorter than its diff:
```python
import functools

import jax
import jax.numpy as jnp
from jax import lax
from jax.experimental import pallas as pl
from jax.experimental.pallas import tpu as pltpu
from jax.sharding import Mesh
from jax.sharding import PartitionSpec as P

HEAD = 128
STEPS = 2
FRAGS = 4
GROUP = 2
WIDE = 256

LEARN_RATE = 0.1
DECAY_RATE = 0.1
BETA_ONE = 0.9
BETA_TWO = 0.999
EPSILON = 1e-08
OUTER_MU = 0.9
OUTER_RATE = 0.7
MERGE_RATE = 0.5
SOFT_CAP = 50.0
QUERY_SCALE = 1.0 / 12.0

FSDP = ("z", "x", "yh")
REPLICA = ("yl", "core")


def shift(array, axis, by):
    size = lax.axis_size(axis)
    return lax.ppermute(array, axis, [(i, (i + by) % size) for i in range(size)])


def dot(a, b, dims):
    return lax.dot_general(a, b, (dims, ((), ())), preferred_element_type=jnp.float32)


def attend(key, query_heads, value, grad_heads, allowed):
    total = None
    for query, grad in zip(query_heads, grad_heads):
        capped = jnp.tanh(dot(key, query, ((1,), (1,))) * (QUERY_SCALE / SOFT_CAP))
        expo = jnp.where(allowed, jnp.exp(SOFT_CAP * capped), 0.0)
        probs = expo * (1.0 / jnp.sum(expo, axis=0, keepdims=True))
        dprob = dot(value, grad, ((1,), (1,)))
        inner = jnp.sum(probs * dprob, axis=0, keepdims=True)
        dscore = (probs * (dprob - inner) * (1.0 - capped * capped)).astype(jnp.bfloat16)
        term = dot(dscore, query, ((1,), (0,)))
        total = term if total is None else total + term
    return (total * QUERY_SCALE).astype(jnp.bfloat16)


def grad_kernel(
    factor, half, f0, f1, ft0, ft1, w, q0, q1, v0, v1, g0, g1, row0, row1, col0, col1, out
):
    weight = w[...]
    dkeys = []
    parts = ((f0, q0, v0, g0, row0, col0), (f1, q1, v1, g1, row1, col1))
    for f, q, v, g, row, col in parts:
        keys = (dot(f[...], weight, ((1,), (0,))) * factor).astype(jnp.bfloat16)
        length = keys.shape[0]
        key_place = lax.broadcasted_iota(jnp.int32, (length, length), 0)
        query_place = lax.broadcasted_iota(jnp.int32, (length, length), 1)
        allowed = (key_place <= query_place) & (row[...] == col[...])
        heads = []
        for h in range(WIDE // HEAD):
            at = lambda ref, i: ref[:, i * HEAD : (i + 1) * HEAD]
            members = range(h * GROUP, (h + 1) * GROUP)
            heads.append(
                attend(
                    keys[:, h * HEAD : (h + 1) * HEAD],
                    [at(q, i) for i in members],
                    at(v, h),
                    [at(g, i) for i in members],
                    allowed,
                )
            )
        dkeys.append(jnp.concatenate(heads, axis=1))
    total = dot(ft0[...], dkeys[0], ((1,), (0,))) + dot(ft1[...], dkeys[1], ((1,), (0,)))
    out[...] = (total * factor).astype(out.dtype)


def weight_term(features, turned, weight, queries, values, grads, docs, half):
    rows, columns = weight.shape
    tokens = features[0].shape[0]
    steps = columns // WIDE
    wide_q = WIDE * GROUP
    whole = lambda shape: pl.BlockSpec(shape, lambda c, half: (0,) * len(shape))
    own = lambda width: pl.BlockSpec((tokens, width), lambda c, half: (0, half[0] * steps + c))
    packed = lambda width, first: pl.BlockSpec(
        (tokens, width), lambda c, half: (0, first // width + c)
    )
    q_end = columns * GROUP
    g_end = 2 * q_end
    kernel = functools.partial(grad_kernel, rows ** (-0.5))
    doc_rows = [doc.reshape(1, tokens) for doc in docs]
    doc_columns = [doc.reshape(tokens, 1) for doc in docs]
    return pl.pallas_call(
        kernel,
        grid_spec=pltpu.PrefetchScalarGridSpec(
            num_scalar_prefetch=1,
            grid=(steps,),
            in_specs=[
                whole((tokens, rows)),
                whole((tokens, rows)),
                whole((rows, tokens)),
                whole((rows, tokens)),
                pl.BlockSpec((rows, WIDE), lambda c, half: (0, c)),
                own(wide_q),
                packed(wide_q, 0),
                own(WIDE),
                packed(WIDE, g_end),
                own(wide_q),
                packed(wide_q, q_end),
                whole((1, tokens)),
                whole((1, tokens)),
                whole((tokens, 1)),
                whole((tokens, 1)),
            ],
            out_specs=pl.BlockSpec((rows, WIDE), lambda c, half: (0, c)),
        ),
        out_shape=jax.ShapeDtypeStruct((rows, columns), jnp.bfloat16),
        compiler_params=pltpu.CompilerParams(vmem_limit_bytes=48 * 1024 * 1024),
        cost_estimate=pl.CostEstimate(
            flops=8 * tokens * rows * columns + 24 * tokens * tokens * columns,
            bytes_accessed=20 * 1024 * 1024,
            transcendentals=8 * tokens * tokens * columns // HEAD,
        ),
    )(
        half,
        *features,
        *turned,
        weight,
        queries[0],
        queries[1],
        values[0],
        values[1],
        grads[0],
        grads[1],
        *doc_rows,
        *doc_columns,
    )


def gather_rows(block):
    x = lax.axis_index("x")
    size = lax.axis_size("x")
    found = [block] + [shift(block, "x", by) for by in range(1, size)]
    turned = jnp.stack([found[(size - i) % size] for i in range(size)] * 2)
    ordered = lax.dynamic_slice_in_dim(turned, (size - x) % size, size, 0)
    ordered = ordered.reshape(size * block.shape[0], block.shape[1])
    return lax.all_gather(ordered, "z", axis=0, tiled=True)


def scatter_rows(term):
    x = lax.axis_index("x")
    size = lax.axis_size("x")
    part = lax.psum_scatter(term, "z", scatter_dimension=0, tiled=True)
    part = part.reshape(size, part.shape[0] // size, part.shape[1])
    total = lax.dynamic_index_in_dim(part, x, 0, False).astype(jnp.float32)
    for by in range(1, size):
        sent = lax.dynamic_index_in_dim(part, (x + by) % size, 0, False)
        total = total + shift(sent, "x", by).astype(jnp.float32)
    return total


def adam(weight, moment, second, grad):
    moment = BETA_ONE * moment + (1.0 - BETA_ONE) * grad
    second = BETA_TWO * second + (1.0 - BETA_TWO) * grad * grad
    weight = weight - LEARN_RATE * (moment / (jnp.sqrt(second) + EPSILON) + DECAY_RATE * weight)
    return weight, moment, second


def outer_merge(fragment, global_weight, outer_momentum, outer_delta):
    frag_cols = global_weight.shape[1] // FRAGS
    start = fragment[0] % FRAGS * frag_cols
    piece = lax.dynamic_slice_in_dim(outer_delta[0], start, frag_cols, 1)
    old_global = lax.dynamic_slice_in_dim(global_weight, start, frag_cols, 1)
    old_moment = lax.dynamic_slice_in_dim(outer_momentum, start, frag_cols, 1)
    count = 1
    for axis in REPLICA:
        piece = piece + shift(piece, axis, 1)
        count *= lax.axis_size(axis)
    mean = piece / count
    fresh_moment = OUTER_MU * old_moment + mean
    fresh_global = old_global - OUTER_RATE * (mean + OUTER_MU * fresh_moment)
    new_global = lax.dynamic_update_slice_in_dim(global_weight, fresh_global, start, 1)
    new_momentum = lax.dynamic_update_slice_in_dim(outer_momentum, fresh_moment, start, 1)
    return (start, fresh_global, new_global, new_momentum)


def on_device(
    features,
    queries,
    values,
    out_grad,
    doc_ids,
    fragment,
    local_weight,
    first_moment,
    second_moment,
    global_weight,
    outer_momentum,
    outer_delta,
):
    yh = lax.axis_index("yh")
    half = yh.astype(jnp.int32).reshape(1)
    columns = local_weight.shape[2] // 2
    owned = local_weight.shape[1]

    def mine(array, wide=columns):
        return lax.dynamic_slice_in_dim(array, yh * wide, wide, array.ndim - 1)

    def theirs(array, wide=columns):
        return lax.dynamic_slice_in_dim(array, (1 - yh) * wide, wide, array.ndim - 1)

    def paired(array):
        got = shift(theirs(array), "yh", 1)
        kept = mine(array)
        first = jnp.where(yh == 0, kept, got)
        last = jnp.where(yh == 0, got, kept)
        return jnp.concatenate([first, last], axis=0)

    weight, moment, second = local_weight[0], first_moment[0], second_moment[0]
    rows = gather_rows(paired(weight.astype(jnp.bfloat16)))

    docs = shift(doc_ids[0], "yh", 1)
    others = []
    for step in range(STEPS):
        pack = jnp.concatenate(
            [
                theirs(queries[0, step], columns * GROUP),
                theirs(out_grad[0, step], columns * GROUP),
                theirs(values[0, step]),
            ],
            axis=1,
        )
        others.append((shift(features[0, step], "yh", 1), shift(pack, "yh", 1)))

    state = None
    for step in range(STEPS):
        other_features, pack = others[step]
        both = (features[0, step], other_features)
        term = weight_term(
            both,
            [f.T for f in both],
            rows,
            (queries[0, step], pack),
            (values[0, step], pack),
            (out_grad[0, step], pack),
            (doc_ids[0, step], docs[step]),
            half,
        )
        grad = scatter_rows(term)
        if step + 1 < STEPS:
            if state is None:
                state = tuple(paired(a) for a in (weight, moment, second))
            state = adam(*state, grad)
            rows = gather_rows(state[0].astype(jnp.bfloat16))
        kept = jnp.where(yh == 0, grad[:owned], grad[owned:])
        sent = jnp.where(yh == 0, grad[owned:], grad[:owned])
        got = shift(sent, "yh", 1)
        left = jnp.where(yh == 0, kept, got)
        right = jnp.where(yh == 0, got, kept)
        own_grad = jnp.concatenate([left, right], axis=1)
        weight, moment, second = adam(weight, moment, second, own_grad)

    outcome = outer_merge(fragment, global_weight, outer_momentum, outer_delta)
    start, fresh_global, new_global, new_momentum = outcome
    frag_cols = fresh_global.shape[1]
    local_frag = lax.dynamic_slice_in_dim(weight, start, frag_cols, 1)
    merged = MERGE_RATE * local_frag + (1.0 - MERGE_RATE) * fresh_global
    weight = lax.dynamic_update_slice_in_dim(weight, merged, start, 1)
    return (weight[None], moment[None], second[None], new_global, new_momentum)


def solution(mesh):
    lattice = Mesh(mesh.devices.reshape(2, 2, 8, 4, 2), REPLICA + FSDP)
    tokens = P(REPLICA, None, FSDP, None)
    shards = P(REPLICA, FSDP, None)
    return jax.shard_map(
        on_device,
        mesh=lattice,
        in_specs=(
            tokens,
            tokens,
            tokens,
            tokens,
            P(REPLICA, None, FSDP),
            P(),
            shards,
            shards,
            shards,
            P(FSDP, None),
            P(FSDP, None),
            shards,
        ),
        out_specs=(shards, shards, shards, P(FSDP, None), P(FSDP, None)),
        check_vma=False,
    )
```

time: 879 us -> 322 us (0.37)
  blocking collectives: 267 us -> 0 us
  waiting for transfers between devices: 438 us -> 189 us
  matrix products: 60.5 us -> 0 us
  local copies, waits for them, and re-layouts: 75.3 us -> 47.8 us
  starting transfers between devices: 10.3 us -> 37.6 us
  Pallas kernels: 0 us -> 24.5 us
    all_gather x2, waiting for transfers between devices: 240 us -> 0.02 us  [gather_rows(): return lax.all_gather(ordered, 'z', axis=0, tiled=True)]
    all_to_all x1 -> x0, blocking collectives: 238 us -> none  [on_device(): lax.all_to_all(whole_term, 'fsdp', split_axis=0, concat_axis=0, tiled=True)]
    all_to_all x1 -> x0, waiting for transfers between devices: 198 us -> none  [on_device(): lax.all_to_all(whole_term, 'fsdp', split_axis=0, concat_axis=0, tiled=True)]
    ppermute x0 -> x25, waiting for transfers between devices: none -> 113 us  [shift(): lax.ppermute(array, axis, [(i, (i + by) % size) for i in range(size)])]
    reduce_scatter x0 -> x2, waiting for transfers between devices: none -> 75.4 us  [scatter_rows(): part = lax.psum_scatter(term, 'z', scatter_dimension=0, tiled=True)]
    dot_general x10 -> x0, matrix products: 52 us -> none  [the longest x2 18.6 us: key_cotangent(): jnp.einsum('kgij,ikgd->jkd', dscore, query_heads, preferred_element_type=...]
    ppermute x0 -> x25, starting transfers between devices: none -> 37.4 us  [shift(): lax.ppermute(array, axis, [(i, (i + by) % size) for i in range(size)])]
    psum x1 -> x0, blocking collectives: 29.9 us -> none  [outer_merge(): mean = lax.psum(piece, 'replica') / lax.axis_size('replica')]
  transfers between devices with their start and end apart: 3 -> 29, of which waited for: 3 -> 17; matrix products, arithmetic and copies ran while one was open for 2% -> 9% of each run, Pallas kernels for 0% -> 0%
where the time goes in v1:
time: 322 us; the launch traced here: 319 us
  waiting for transfers between devices  189 us (59%)
  local copies, waits for them, and re-layouts  47.8 us (15%)
  starting transfers between devices  37.6 us (12%)
  Pallas kernels  24.5 us (8%)
  between operations  15 us (5%)
  other arithmetic  5.59 us (2%)
    ppermute x25, waiting for transfers between devices, shift(): lax.ppermute(array, axis, [(i, (i + by) % size) for i in range(size)])  113 us
    reduce_scatter x2, waiting for transfers between devices, scatter_rows(): part = lax.psum_scatter(term, 'z', scatter_dimension=0, tiled=True)  75.4 us
    ppermute x25, starting transfers between devices, shift(): lax.ppermute(array, axis, [(i, (i + by) % size) for i in range(size)])  37.4 us
    pallas_call x2, Pallas kernels, weight_term(): pl.pallas_call(kernel, grid_spec=pltpu.PrefetchScalarGridSpec(num_scalar_...  24.5 us
    unnamed x86, local copies, waits for them, and re-layouts  22.9 us
    another operation x6, local copies, waits for them, and re-layouts, weight_term(): doc_columns = [doc.reshape(tokens, 1) for doc in docs]  8.43 us
  transfers between devices with their start and end apart: 29, of which 17 were waited for; matrix products, arithmetic and copies ran while one was open for 9% of the time, Pallas kernels for 0%

profile of v1, /device:TPU:26, one launch (start us, length us, event | category | flops | bytes accessed | tf_op | source)
XLA Modules:
  0.0 319.2 jit_solution(3908343521408957496)
XLA Ops:
  7.2 1.0 copy.109
  8.3 1.3 collective-permute-start.1
  9.6 4.3 %collective-permute-done.1 = bf16[36,512]{1,0:T(8,128)(2,1)S(1)} collective-permute-done((bf16[36,512]{1,0:T(8,128)(2,1)S(1)}, bf16[36,512]{1,0:T(8,128)(2,1)S(1)}, u32[]{:S(2)}, u32[]{:S(2)}) %collective-permute-start.1) | collective-permute-done | bytes 36896 | tf_op jit(solution)/shard_map/ppermute | solution.py:34
  14.5 1.5 collective-permute-start.4
  16.0 3.3 %collective-permute-start.3 = (bf16[72,512]{1,0:T(8,128)(2,1)S(1)}, bf16[72,512]{1,0:T(8,128)(2,1)S(1)}, u32[]{:S(2)}, u32[]{:S(2)}) collective-permute-start(bf16[72,512]{1,0:T(8,128)(2,1)S(1)} %get-tuple-element.21), channel_id=1, source_target_pairs={{0,4},{2,6},{4,0},{6,2},{1,5},{3,7},{5,1},{7,3},{8,12},{10,14},{12... | collective-permute-start | bytes 221192 | tf_op jit(solution)/shard_map/ppermute | solution.py:34
  19.4 2.5 collective-permute-done.3
  22.8 1.3 slice_bitcast_fusion.6
  25.0 1.8 fusion.29
  27.0 1.9 slice_bitcast_fusion.8
  29.0 1.2 pad_maximum_fusion
  30.2 1.2 collective-permute-start.5
  31.4 1.8 fusion.28
  33.2 2.4 copy.55
  35.6 2.3 collective-permute-start
  37.9 1.2 collective-permute-start.6
  39.1 1.3 slice_bitcast_fusion
  40.4 1.5 copy.34.col0
  41.9 43.8 %collective-permute-done.6 = s32[2,256]{1,0:T(2,128)} collective-permute-done((s32[2,256]{1,0:T(2,128)}, s32[2,256]{1,0:T(2,128)}, u32[]{:S(2)}, u32[]{:S(2)}) %collective-permute-start.6) | collective-permute-done | bytes 2080 | tf_op jit(solution)/shard_map/ppermute | solution.py:34
  85.7 1.3 slice_bitcast_fusion.4
  87.0 1.4 copy.35.col1
  88.4 2.4 copy.33.f1
  90.8 1.3 copy-done.1
  92.0 1.2 copy-done.3
  93.3 1.2 copy-done.4
  94.5 1.0 copy-done.6
  98.7 12.3 %shard_map.155 = bf16[2304,512]{1,0:T(8,128)(2,1)} custom-call(s32[1]{0:T(128)} %bitcast.half, bf16[256,2304]{1,0:T(8,128)(2,1)S(1)} %get-tuple-element.23.f0, bf16[256,2304]{1,0:T(8,128)(2,1)S(1)} %copy-done.1, bf16[2304,256]{1,0:T(8,128)(2,1)} %bitcast.148, bf16[2304,256]{1,0:T(8,128)(2,1)} %bitcast.3.ft1, ...), custom_call_target="tpu_custom_call" | custom-call | flops 3221225472 | bytes 20971520 | tf_op jit(solution)/shard_map/pallas_call | solution.py:100
  111.9 1.3 collective-permute-start.12
  113.5 2.4 collective-permute-start.13
  115.9 1.2 collective-permute-start.14
  118.0 1.5 collective-permute-done.13
  119.5 37.6 %reduce-scatter.3.cloned.1.call-done = bf16[288,512]{1,0:T(8,128)(2,1)} async-done(((bf16[2304,512]{1,0:T(8,128)(2,1)}), bf16[288,512]{1,0:T(8,128)(2,1)}) %reduce-scatter.3.cloned.1.call-update) | async-done | bytes 294928 | tf_op jit(solution)/shard_map/reduce_scatter | solution.py:160
  157.1 1.0 dynamic-slice_bitcast_fusion.11
  158.1 1.6 collective-permute-start.7
  160.2 2.1 collective-permute-start.8
  162.5 1.5 collective-permute-done.9
  164.0 2.8 collective-permute-done.8
  166.8 1.7 bitcast_dynamic-update-slice_fusion.6
  168.5 1.4 collective-permute-start.15
  170.5 3.1 collective-permute-start.16
  173.6 2.8 collective-permute-done.16
  177.3 1.0 dynamic-slice_bitcast_fusion.4
  178.3 1.1 dynamic-slice_bitcast_fusion
  179.4 1.2 pad_maximum_fusion.1
  180.5 1.4 collective-permute-start.18
  182.0 1.6 copy.56
  183.6 2.2 collective-permute-start.11
  185.8 1.5 copy.42.col0
  187.2 1.4 copy.43.col1
  188.7 41.5 %collective-permute-done.11 = bf16[256,2304]{0,1:T(8,128)(2,1)} collective-permute-done((bf16[256,2304]{0,1:T(8,128)(2,1)S(1)}, bf16[256,2304]{0,1:T(8,128)(2,1)}, u32[]{:S(2)}, u32[]{:S(2)}) %collective-permute-start.11) | collective-permute-done | bytes 1179680 | tf_op jit(solution)/shard_map/ppermute | solution.py:34
  230.1 1.6 copy.41.f1
  231.8 1.2 copy-done.2
  233.0 1.0 copy-done.5
  237.2 12.3 %shard_map.156 = bf16[2304,512]{1,0:T(8,128)(2,1)} custom-call(s32[1]{0:T(128)} %bitcast.half, bf16[256,2304]{1,0:T(8,128)(2,1)S(1)} %get-tuple-element.24.f0, bf16[256,2304]{1,0:T(8,128)(2,1)S(1)} %copy.41.f1, bf16[2304,256]{1,0:T(8,128)(2,1)} %bitcast.150, bf16[2304,256]{1,0:T(8,128)(2,1)} %bitcast.28.ft1, ...), custom_call_target="tpu_custom_call" | custom-call | flops 3221225472 | bytes 20971520 | tf_op jit(solution)/shard_map/pallas_call | solution.py:100
  251.2 3.2 collective-permute-done.23
  254.4 1.2 collective-permute-done.24
  255.7 37.9 %reduce-scatter.5.cloned.1.call-done = bf16[288,512]{1,0:T(8,128)(2,1)} async-done(((bf16[2304,512]{1,0:T(8,128)(2,1)}), bf16[288,512]{1,0:T(8,128)(2,1)}) %reduce-scatter.5.cloned.1.call-update) | async-done | bytes 294928 | tf_op jit(solution)/shard_map/reduce_scatter | solution.py:160
  293.5 1.0 dynamic-slice_bitcast_fusion.8
  294.5 1.6 collective-permute-start.19
  296.8 2.0 collective-permute-start.20
  298.9 1.4 collective-permute-start.10
  300.4 2.2 collective-permute-done.20
  302.7 0.9 fusion.13
  303.6 1.4 collective-permute-start.22
  305.0 4.7 %collective-permute-done.22 = f32[36,512]{1,0:T(8,128)S(1)} collective-permute-done((f32[36,512]{1,0:T(8,128)S(1)}, f32[36,512]{1,0:T(8,128)S(1)}, u32[]{:S(2)}, u32[]{:S(2)}) %collective-permute-start.22) | collective-permute-done | bytes 73760 | tf_op jit(solution)/shard_map/ppermute | solution.py:34
  (130 shorter events, 18.4 us)
Async XLA Ops:
  7.2 243.0 %copy-start = (f32[1,36,1024]{2,0,1:T(1,128)S(1)}, f32[1,36,1024]{2,0,1:T(1,128)}, u32[]{:S(2)}) copy-start(f32[1,36,1024]{2,0,1:T(1,128)} %param.23) | copy-start | bytes 442372
  7.2 83.6 %all-gather.3.cloned.1.call-start = ((), (), s32[]{:S(2)}) async-start(), calls=%async_computation.2 | async-start | bytes 2654208 | tf_op jit(solution)/shard_map/all_gather | solution.py:154
  7.2 15.6 %copy-start.27 = (bf16[1,2,256,1024]{3,2,1,0:T(8,128)(2,1)S(1)}, bf16[1,2,256,1024]{3,2,1,0:T(8,128)(2,1)}, u32[]{:S(2)}) copy-start(bf16[1,2,256,1024]{3,2,1,0:T(8,128)(2,1)} %param.14) | copy-start | bytes 3145732
  8.3 5.6 %collective-permute-start.1 = (bf16[36,512]{1,0:T(8,128)(2,1)S(1)}, bf16[36,512]{1,0:T(8,128)(2,1)S(1)}, u32[]{:S(2)}, u32[]{:S(2)}) collective-permute-start(bf16[36,512]{1,0:T(8,128)(2,1)S(1)} %constant_dynamic-slice_fusion.9), channel_id=1, source_target_pairs={{0,1},{1,0},{2,3},{3,2},{4,5},{5,4},{6,7},{7,6},{8,9},{9,8},{10,11... | collective-permute-start | bytes 110600 | tf_op jit(solution)/shard_map/ppermute | solution.py:34
  13.9 5.4 %collective-permute-start.2 = (bf16[72,512]{1,0:T(8,128)(2,1)S(1)}, bf16[72,512]{1,0:T(8,128)(2,1)S(1)}, u32[]{:S(2)}, u32[]{:S(2)}) collective-permute-start(bf16[72,512]{1,0:T(8,128)(2,1)S(1)} %get-tuple-element.21), channel_id=1, source_target_pairs={{0,6},{2,0},{4,2},{6,4},{1,7},{3,1},{5,3},{7,5},{8,14},{10,8},{12,... | collective-permute-start | bytes 221192 | tf_op jit(solution)/shard_map/ppermute | solution.py:34
  14.5 7.4 %collective-permute-start.4 = (bf16[72,512]{1,0:T(8,128)(2,1)S(1)}, bf16[72,512]{1,0:T(8,128)(2,1)S(1)}, u32[]{:S(2)}, u32[]{:S(2)}) collective-permute-start(bf16[72,512]{1,0:T(8,128)(2,1)S(1)} %get-tuple-element.21), channel_id=1, source_target_pairs={{0,2},{2,4},{4,6},{6,0},{1,3},{3,5},{5,7},{7,1},{8,10},{10,12},{12... | collective-permute-start | bytes 221192 | tf_op jit(solution)/shard_map/ppermute | solution.py:34
  16.0 5.9 %collective-permute-start.3 = (bf16[72,512]{1,0:T(8,128)(2,1)S(1)}, bf16[72,512]{1,0:T(8,128)(2,1)S(1)}, u32[]{:S(2)}, u32[]{:S(2)}) collective-permute-start(bf16[72,512]{1,0:T(8,128)(2,1)S(1)} %get-tuple-element.21), channel_id=1, source_target_pairs={{0,4},{2,6},{4,0},{6,2},{1,5},{3,7},{5,1},{7,3},{8,12},{10,14},{12... | collective-permute-start | bytes 221192 | tf_op jit(solution)/shard_map/ppermute | solution.py:34
  22.8 134.3 %reduce-scatter.3.cloned.1.call-start = ((), (), s32[]{:S(2)}) async-start(), calls=%async_computation.3 | async-start | bytes 2654208 | tf_op jit(solution)/shard_map/reduce_scatter | solution.py:160
  22.8 2.2 copy-start.20
  25.0 2.0 copy-start.21
  29.0 2.4 copy-start.16
  30.2 60.6 %collective-permute-start.5 = (bf16[256,2560]{1,0:T(8,128)(2,1)}, bf16[256,2560]{1,0:T(8,128)(2,1)}, u32[]{:S(2)}, u32[]{:S(2)}) collective-permute-start(bf16[256,2560]{1,0:T(8,128)(2,1)} %pad_maximum_fusion), channel_id=1, source_target_pairs={{0,1},{1,0},{2,3},{3,2},{4,5},{5,4},{6,7},{7,6},{8,9},{9,8},{10,11... | collective-permute-start | bytes 3932168 | tf_op jit(solution)/shard_map/ppermute | solution.py:34
  35.6 52.8 %collective-permute-start = (bf16[256,2304]{0,1:T(8,128)(2,1)}, bf16[256,2304]{0,1:T(8,128)(2,1)}, u32[]{:S(2)}, u32[]{:S(2)}) collective-permute-start(bf16[256,2304]{0,1:T(8,128)(2,1)} %bitcast.147), channel_id=1, source_target_pairs={{0,1},{1,0},{2,3},{3,2},{4,5},{5,4},{6,7},{7,6},{8,9},{9,8},{10,11... | collective-permute-start | bytes 3538952 | tf_op jit(solution)/shard_map/ppermute | solution.py:34
  37.9 47.8 %collective-permute-start.6 = (s32[2,256]{1,0:T(2,128)}, s32[2,256]{1,0:T(2,128)}, u32[]{:S(2)}, u32[]{:S(2)}) collective-permute-start(s32[2,256]{1,0:T(2,128)} %bitcast.167), channel_id=1, source_target_pairs={{0,1},{1,0},{2,3},{3,2},{4,5},{5,4},{6,7},{7,6},{8,9},{9,8},{10,11... | collective-permute-start | bytes 6152 | tf_op jit(solution)/shard_map/ppermute | solution.py:34
  90.8 1.3 copy-start.1
  92.0 1.2 copy-start.3
  93.3 1.2 copy-start.4
  94.5 1.0 copy-start.6
  95.5 0.9 copy-start.7
  96.4 0.9 copy-start.10
  97.3 0.7 copy-start.13
  98.0 0.7 copy-start.14
  111.0 0.9 copy-start.17
  111.0 2.3 copy-start.23
  111.0 2.3 copy-start.25
  111.0 120.7 %all-gather.5.cloned.1.call-start = ((), (), s32[]{:S(2)}) async-start(), calls=%async_computation.4 | async-start | bytes 2654208 | tf_op jit(solution)/shard_map/all_gather | solution.py:154
  111.9 6.0 %collective-permute-start.12 = (f32[36,512]{1,0:T(8,128)S(1)}, f32[36,512]{1,0:T(8,128)S(1)}, u32[]{:S(2)}, u32[]{:S(2)}) collective-permute-start(f32[36,512]{1,0:T(8,128)S(1)} %bitcast.164), channel_id=1, source_target_pairs={{0,1},{1,0},{2,3},{3,2},{4,5},{5,4},{6,7},{7,6},{8,9},{9,8},{10,11... | collective-permute-start | bytes 221192 | tf_op jit(solution)/shard_map/ppermute | solution.py:34
  113.5 6.0 %collective-permute-start.13 = (f32[36,512]{1,0:T(8,128)S(1)}, f32[36,512]{1,0:T(8,128)S(1)}, u32[]{:S(2)}, u32[]{:S(2)}) collective-permute-start(f32[36,512]{1,0:T(8,128)S(1)} %bitcast.165), channel_id=1, source_target_pairs={{0,1},{1,0},{2,3},{3,2},{4,5},{5,4},{6,7},{7,6},{8,9},{9,8},{10,11... | collective-permute-start | bytes 221192 | tf_op jit(solution)/shard_map/ppermute | solution.py:34
  115.9 46.4 %collective-permute-start.14 = (f32[36,512]{1,0:T(8,128)S(1)}, f32[36,512]{1,0:T(8,128)S(1)}, u32[]{:S(2)}, u32[]{:S(2)}) collective-permute-start(f32[36,512]{1,0:T(8,128)S(1)} %bitcast.163), channel_id=1, source_target_pairs={{0,1},{1,0},{2,3},{3,2},{4,5},{5,4},{6,7},{7,6},{8,9},{9,8},{10,11... | collective-permute-start | bytes 221192 | tf_op jit(solution)/shard_map/ppermute | solution.py:34
  158.1 4.4 %collective-permute-start.7 = (bf16[72,512]{1,0:T(8,128)(2,1)S(1)}, bf16[72,512]{1,0:T(8,128)(2,1)S(1)}, u32[]{:S(2)}, u32[]{:S(2)}) collective-permute-start(bf16[72,512]{1,0:T(8,128)(2,1)S(1)} %get-tuple-element.47), channel_id=1, source_target_pairs={{0,2},{2,4},{4,6},{6,0},{1,3},{3,5},{5,7},{7,1},{8,10},{10,12},{12... | collective-permute-start | bytes 221192 | tf_op jit(solution)/shard_map/ppermute | solution.py:34
  159.6 4.4 %collective-permute-start.9 = (bf16[72,512]{1,0:T(8,128)(2,1)S(1)}, bf16[72,512]{1,0:T(8,128)(2,1)S(1)}, u32[]{:S(2)}, u32[]{:S(2)}) collective-permute-start(bf16[72,512]{1,0:T(8,128)(2,1)S(1)} %get-tuple-element.48), channel_id=1, source_target_pairs={{0,6},{2,0},{4,2},{6,4},{1,7},{3,1},{5,3},{7,5},{8,14},{10,8},{12,... | collective-permute-start | bytes 221192 | tf_op jit(solution)/shard_map/ppermute | solution.py:34
  160.2 6.6 %collective-permute-start.8 = (bf16[72,512]{1,0:T(8,128)(2,1)S(1)}, bf16[72,512]{1,0:T(8,128)(2,1)S(1)}, u32[]{:S(2)}, u32[]{:S(2)}) collective-permute-start(bf16[72,512]{1,0:T(8,128)(2,1)S(1)} %get-tuple-element.49), channel_id=1, source_target_pairs={{0,4},{2,6},{4,0},{6,2},{1,5},{3,7},{5,1},{7,3},{8,12},{10,14},{12... | collective-permute-start | bytes 221192 | tf_op jit(solution)/shard_map/ppermute | solution.py:34
  168.5 9.8 %copy-start.19 = (bf16[1,1,256,2048]{3,2,1,0:T(8,128)(2,1)S(1)}, bf16[1,1,256,2048]{3,2,1,0:T(8,128)(2,1)}, u32[]{:S(2)}) copy-start(bf16[1,1,256,2048]{3,2,1,0:T(8,128)(2,1)} %get-tuple-element.30) | copy-start | bytes 3145732
  168.5 5.1 %collective-permute-start.15 = (bf16[72,512]{1,0:T(8,128)(2,1)S(1)}, bf16[72,512]{1,0:T(8,128)(2,1)S(1)}, u32[]{:S(2)}, u32[]{:S(2)}) collective-permute-start(bf16[72,512]{1,0:T(8,128)(2,1)S(1)} %get-tuple-element.18), channel_id=1, source_target_pairs={{0,6},{2,0},{4,2},{6,4},{1,7},{3,1},{5,3},{7,5},{8,14},{10,8},{12,... | collective-permute-start | bytes 221192 | tf_op jit(solution)/shard_map/ppermute | solution.py:34
  169.9 6.5 %collective-permute-start.17 = (bf16[72,512]{1,0:T(8,128)(2,1)S(1)}, bf16[72,512]{1,0:T(8,128)(2,1)S(1)}, u32[]{:S(2)}, u32[]{:S(2)}) collective-permute-start(bf16[72,512]{1,0:T(8,128)(2,1)S(1)} %get-tuple-element.18), channel_id=1, source_target_pairs={{0,2},{2,4},{4,6},{6,0},{1,3},{3,5},{5,7},{7,1},{8,10},{10,12},{12... | collective-permute-start | bytes 221192 | tf_op jit(solution)/shard_map/ppermute | solution.py:34
  170.5 5.9 %collective-permute-start.16 = (bf16[72,512]{1,0:T(8,128)(2,1)S(1)}, bf16[72,512]{1,0:T(8,128)(2,1)S(1)}, u32[]{:S(2)}, u32[]{:S(2)}) collective-permute-start(bf16[72,512]{1,0:T(8,128)(2,1)S(1)} %get-tuple-element.18), channel_id=1, source_target_pairs={{0,4},{2,6},{4,0},{6,2},{1,5},{3,7},{5,1},{7,3},{8,12},{10,14},{12... | collective-permute-start | bytes 221192 | tf_op jit(solution)/shard_map/ppermute | solution.py:34
  177.2 116.3 %reduce-scatter.5.cloned.1.call-start = ((), (), s32[]{:S(2)}) async-start(), calls=%async_computation.5 | async-start | bytes 2654208 | tf_op jit(solution)/shard_map/reduce_scatter | solution.py:160
  180.5 51.2 %collective-permute-start.18 = (bf16[256,2560]{1,0:T(8,128)(2,1)}, bf16[256,2560]{1,0:T(8,128)(2,1)}, u32[]{:S(2)}, u32[]{:S(2)}) collective-permute-start(bf16[256,2560]{1,0:T(8,128)(2,1)} %pad_maximum_fusion.1), channel_id=1, source_target_pairs={{0,1},{1,0},{2,3},{3,2},{4,5},{5,4},{6,7},{7,6},{8,9},{9,8},{10,11... | collective-permute-start | bytes 3932168 | tf_op jit(solution)/shard_map/ppermute | solution.py:34
  183.6 5.1 %copy-start.15 = (bf16[1,1,256,2304]{2,3,1,0:T(8,128)(2,1)}, bf16[1,1,256,2304]{2,3,1,0:T(8,128)(2,1)S(1)}, u32[]{:S(2)}) copy-start(bf16[1,1,256,2304]{2,3,1,0:T(8,128)(2,1)S(1)} %copy.56) | copy-start | bytes 3538948
  183.6 46.6 %collective-permute-start.11 = (bf16[256,2304]{0,1:T(8,128)(2,1)S(1)}, bf16[256,2304]{0,1:T(8,128)(2,1)}, u32[]{:S(2)}, u32[]{:S(2)}) collective-permute-start(bf16[256,2304]{0,1:T(8,128)(2,1)S(1)} %bitcast.149), channel_id=1, source_target_pairs={{0,1},{1,0},{2,3},{3,2},{4,5},{5,4},{6,7},{7,6},{8,9},{9,8},{10,11... | collective-permute-start | bytes 3538952 | tf_op jit(solution)/shard_map/ppermute | solution.py:34
  231.8 1.2 copy-start.2
  233.0 1.0 copy-start.5
  234.0 0.9 copy-start.8
  234.9 0.9 copy-start.9
  235.8 0.7 copy-start.11
  236.5 0.7 copy-start.12
  249.4 6.2 %copy-start.29 = (f32[36,1024]{1,0:T(8,128)S(1)}, f32[36,1024]{1,0:T(8,128)}, u32[]{:S(2)}) copy-start(f32[36,1024]{1,0:T(8,128)} %param.21) | copy-start | bytes 442372
  249.4 6.2 %copy-start.31 = (f32[36,1024]{1,0:T(8,128)S(1)}, f32[36,1024]{1,0:T(8,128)}, u32[]{:S(2)}) copy-start(f32[36,1024]{1,0:T(8,128)} %param.22) | copy-start | bytes 442372
  249.4 49.4 %copy-start.22 = (f32[72,512]{1,0:T(8,128)S(1)}, f32[72,512]{1,0:T(8,128)}, u32[]{:S(2)}) copy-start(f32[72,512]{1,0:T(8,128)} %get-tuple-element.19) | copy-start | bytes 442372
  250.2 59.4 %copy-start.18 = (f32[1,36,1024]{2,0,1:T(1,128)S(1)}, f32[1,36,1024]{2,0,1:T(1,128)}, u32[]{:S(2)}) copy-start(f32[1,36,1024]{2,0,1:T(1,128)} %param.18) | copy-start | bytes 442372
  250.3 59.4 %copy-start.24 = (f32[1,36,1024]{2,0,1:T(1,128)S(1)}, f32[1,36,1024]{2,0,1:T(1,128)}, u32[]{:S(2)}) copy-start(f32[1,36,1024]{2,0,1:T(1,128)} %param.20) | copy-start | bytes 442372
  250.3 59.4 %copy-start.26 = (f32[1,36,1024]{2,0,1:T(1,128)S(1)}, f32[1,36,1024]{2,0,1:T(1,128)}, u32[]{:S(2)}) copy-start(f32[1,36,1024]{2,0,1:T(1,128)} %param.19) | copy-start | bytes 442372
  250.3 4.1 %collective-permute-start.23 = (f32[36,256]{1,0:T(8,128)S(1)}, f32[36,256]{1,0:T(8,128)S(1)}, u32[]{:S(2)}, u32[]{:S(2)}) collective-permute-start(f32[36,256]{1,0:T(8,128)S(1)} %bitcast.166), channel_id=1, source_target_pairs={{0,128},{128,0},{1,129},{129,1},{2,130},{130,2},{3,131},{131,3},{4... | collective-permute-start | bytes 110600 | tf_op jit(solution)/shard_map/ppermute | solution.py:34
  254.4 1.2 collective-permute-start.24
  255.6 54.3 %copy-start.28 = (f32[36,1024]{1,0:T(8,128)}, f32[36,1024]{1,0:T(8,128)S(1)}, u32[]{:S(2)}) copy-start(f32[36,1024]{1,0:T(8,128)S(1)} %get-tuple-element.15) | copy-start | bytes 442372
  255.6 54.3 %copy-start.30 = (f32[36,1024]{1,0:T(8,128)}, f32[36,1024]{1,0:T(8,128)S(1)}, u32[]{:S(2)}) copy-start(f32[36,1024]{1,0:T(8,128)S(1)} %get-tuple-element.50) | copy-start | bytes 442372
  294.5 5.8 %collective-permute-start.19 = (bf16[72,512]{1,0:T(8,128)(2,1)S(1)}, bf16[72,512]{1,0:T(8,128)(2,1)S(1)}, u32[]{:S(2)}, u32[]{:S(2)}) collective-permute-start(bf16[72,512]{1,0:T(8,128)(2,1)S(1)} %get-tuple-element.44), channel_id=1, source_target_pairs={{0,2},{2,4},{4,6},{6,0},{1,3},{3,5},{5,7},{7,1},{8,10},{10,12},{12... | collective-permute-start | bytes 221192 | tf_op jit(solution)/shard_map/ppermute | solution.py:34
  296.1 4.4 %collective-permute-start.21 = (bf16[72,512]{1,0:T(8,128)(2,1)S(1)}, bf16[72,512]{1,0:T(8,128)(2,1)S(1)}, u32[]{:S(2)}, u32[]{:S(2)}) collective-permute-start(bf16[72,512]{1,0:T(8,128)(2,1)S(1)} %get-tuple-element.45), channel_id=1, source_target_pairs={{0,6},{2,0},{4,2},{6,4},{1,7},{3,1},{5,3},{7,5},{8,14},{10,8},{12,... | collective-permute-start | bytes 221192 | tf_op jit(solution)/shard_map/ppermute | solution.py:34
  296.8 5.9 %collective-permute-start.20 = (bf16[72,512]{1,0:T(8,128)(2,1)S(1)}, bf16[72,512]{1,0:T(8,128)(2,1)S(1)}, u32[]{:S(2)}, u32[]{:S(2)}) collective-permute-start(bf16[72,512]{1,0:T(8,128)(2,1)S(1)} %get-tuple-element.46), channel_id=1, source_target_pairs={{0,4},{2,6},{4,0},{6,2},{1,5},{3,7},{5,1},{7,3},{8,12},{10,14},{12... | collective-permute-start | bytes 221192 | tf_op jit(solution)/shard_map/ppermute | solution.py:34
  298.9 6.1 %collective-permute-start.10 = (f32[36,512]{1,0:T(8,128)S(1)}, f32[36,512]{1,0:T(8,128)S(1)}, u32[]{:S(2)}, u32[]{:S(2)}) collective-permute-start(f32[36,512]{1,0:T(8,128)S(1)} %slice_select_fusion.2), channel_id=1, source_target_pairs={{0,1},{1,0},{2,3},{3,2},{4,5},{5,4},{6,7},{7,6},{8,9},{9,8},{10,11... | collective-permute-start | bytes 221192 | tf_op jit(solution)/shard_map/ppermute | solution.py:34
  303.6 6.0 %collective-permute-start.22 = (f32[36,512]{1,0:T(8,128)S(1)}, f32[36,512]{1,0:T(8,128)S(1)}, u32[]{:S(2)}, u32[]{:S(2)}) collective-permute-start(f32[36,512]{1,0:T(8,128)S(1)} %slice_select_fusion), channel_id=1, source_target_pairs={{0,1},{1,0},{2,3},{3,2},{4,5},{5,4},{6,7},{7,6},{8,9},{9,8},{10,11... | collective-permute-start | bytes 221192 | tf_op jit(solution)/shard_map/ppermute | solution.py:34
Sparse Core Ops, SparseCore 0:
  22.9 45.0 all-gather.2
  111.1 45.9 reduce-scatter.2
  177.4 40.8 all-gather.4
  249.6 43.8 reduce-scatter.4
